TPU v7x, 32 devices: a whole 2x2x4 slice. The times are simulated.
32 devices in a mesh: groups: 2 (over x), hid: 16 (over z, y, core).
Axes of the slice: x: 2, y: 2, z: 4, core: 2. Of those that a mesh axis runs over, the one named last changes fastest.
Arguments:
- tokens: bfloat16 [2, 32, 8192], P(None, ('groups', 'hid')), parts along dimension 1, may hold values from -6 to 6
- positions: int32 [32], P(('groups', 'hid')), parts along dimension 0, may hold values from 0 to 8191
- lengths: int32 [32], P(('groups', 'hid')), parts along dimension 0, may hold values from 64 to 510, as said below
- w_query: bfloat16 [8192, 8192], P(None, 'hid'), may hold values from -0.0625 to 0.0625
- w_key: bfloat16 [8192, 1024], P(None, 'hid'), may hold values from -0.0625 to 0.0625
- w_value: bfloat16 [8192, 1024], P(None, 'hid'), may hold values from -0.0625 to 0.0625
- w_out: bfloat16 [8192, 8192], P('hid'), may hold values from -1.5 to 1.5
- cache_keys: bfloat16 [32, 512, 1024], P(('groups', 'hid')), parts along dimension 0, may hold values from -128 to 128
- cache_values: bfloat16 [32, 512, 1024], P(('groups', 'hid')), parts along dimension 0, may hold values from -4 to 4
Outputs:
- attended: bfloat16 [2, 32, 8192], P(None, ('groups', 'hid')), parts along dimension 1
There are 2 independent parts, one for each index of `groups`. A program takes and returns all parts, laid end to end along the dimension named above; an argument that names none is the same for every part. Nothing has to cross between parts.
Inputs may be any that keep to these rules, and one draw needn't show every extreme that they name: Row r's cache holds valid keys and values at positions 0 to lengths[r] - 1; some row has length 510.
All inputs are finite; a program needn't handle non-finite values.
Results may differ from a plain program's by a relative error of at most 0.012.
Values may be sent and summed in bfloat16 or wider, within the bound.
A program may use at most 128 MiB of HBM per device.

v0:
```python
import math

import jax
import jax.numpy as jnp
from jax import lax
from jax.sharding import PartitionSpec as P

HEADS = 64
KV_HEADS = 8
HEAD = 128
GROUP = HEADS // KV_HEADS


def normalize(values):
    widened = values.astype(jnp.float32)
    factor = lax.rsqrt(jnp.mean(widened * widened, axis=-1, keepdims=True) + 1e-06)
    return (widened * factor).astype(jnp.bfloat16)


def rotate(values, places):
    half_width = values.shape[-1] // 2
    inverse = jnp.exp(
        jnp.arange(half_width, dtype=jnp.float32) * (-2.0 * math.log(1000000.0) / values.shape[-1])
    )
    angles = places.astype(jnp.float32)[..., None, None] * inverse
    cosine = jnp.cos(angles)
    sine = jnp.sin(angles)
    first_half = values[..., :half_width]
    second_half = values[..., half_width:]
    return jnp.concatenate(
        [first_half * cosine - second_half * sine, second_half * cosine + first_half * sine],
        axis=-1,
    )


def per_device(
    tokens, positions, lengths, w_query, w_key, w_value, w_out, cache_keys, cache_values
):
    size = lax.axis_size("hid")
    steps, _, width = tokens.shape
    capacity = cache_keys.shape[1]
    query_width = w_query.shape[1]
    key_width = w_key.shape[1]
    normed = normalize(tokens[:, 0])
    rows = lax.all_gather(normed, "hid", axis=0, tiled=True)
    parts = [
        jnp.dot(rows, w, preferred_element_type=jnp.float32).astype(jnp.bfloat16)
        for w in (w_query, w_key, w_value)
    ]
    columns = jnp.concatenate(parts, axis=-1).reshape(size, steps, -1)
    mine = lax.all_to_all(columns, "hid", split_axis=0, concat_axis=0, tiled=True)
    mine = jnp.transpose(mine, (1, 0, 2))
    query = mine[..., :query_width].reshape(steps, HEADS, HEAD)
    key = mine[..., query_width : query_width + key_width].reshape(steps, KV_HEADS, HEAD)
    value = mine[..., query_width + key_width :].reshape(steps, KV_HEADS, HEAD)
    places = positions + jnp.arange(steps, dtype=jnp.int32)
    query = rotate(query.astype(jnp.float32), places).astype(jnp.bfloat16)
    key = rotate(key.astype(jnp.float32), places).astype(jnp.bfloat16)
    grouped = query.reshape(steps, KV_HEADS, GROUP, HEAD)
    keys_cached = cache_keys[0].reshape(capacity, KV_HEADS, HEAD)
    values_cached = cache_values[0].reshape(capacity, KV_HEADS, HEAD)
    scale = HEAD ** (-0.5)
    scores_cached = (
        jnp.einsum("skgd,ckd->kgsc", grouped, keys_cached, preferred_element_type=jnp.float32)
        * scale
    )
    valid = jnp.arange(capacity, dtype=jnp.int32) < lengths[0]
    scores_cached = jnp.where(valid, scores_cached, -jnp.inf)
    scores_new = (
        jnp.einsum("skgd,nkd->kgsn", grouped, key, preferred_element_type=jnp.float32) * scale
    )
    seen = jnp.arange(steps)[None, :] <= jnp.arange(steps)[:, None]
    scores_new = jnp.where(seen, scores_new, -jnp.inf)
    highest = jnp.maximum(jnp.max(scores_cached, axis=-1), jnp.max(scores_new, axis=-1))
    exp_cached = jnp.exp(scores_cached - highest[..., None])
    exp_new = jnp.exp(scores_new - highest[..., None])
    total = jnp.sum(exp_cached, axis=-1) + jnp.sum(exp_new, axis=-1)
    weights_cached = (exp_cached / total[..., None]).astype(jnp.bfloat16)
    weights_new = (exp_new / total[..., None]).astype(jnp.bfloat16)
    mixed = jnp.einsum(
        "kgsc,ckd->skgd", weights_cached, values_cached, preferred_element_type=jnp.float32
    )
    mixed = mixed + jnp.einsum(
        "kgsn,nkd->skgd", weights_new, value, preferred_element_type=jnp.float32
    )
    mixed = mixed.astype(jnp.bfloat16).reshape(steps, size, query_width)
    mixed = jnp.transpose(mixed, (1, 0, 2))
    heads = lax.all_to_all(mixed, "hid", split_axis=0, concat_axis=0, tiled=True)
    product = jnp.dot(
        heads.reshape(size * steps, query_width), w_out, preferred_element_type=jnp.float32
    )
    summed = lax.psum_scatter(product, "hid", scatter_dimension=0, tiled=True)
    return summed.astype(jnp.bfloat16)[:, None]


def solution(mesh):
    return jax.shard_map(
        per_device,
        mesh=mesh,
        in_specs=(
            P(None, ("groups", "hid"), None),
            P(("groups", "hid")),
            P(("groups", "hid")),
            P(None, "hid"),
            P(None, "hid"),
            P(None, "hid"),
            P("hid", None),
            P(("groups", "hid"), None, None),
            P(("groups", "hid"), None, None),
        ),
        out_specs=P(None, ("groups", "hid"), None),
        check_vma=False,
    )
```

profile of v0, /device:TPU:0, one launch (start us, length us, event | category | flops | bytes accessed | tf_op | source)
XLA Modules:
  0.0 131.4 jit_solution(9413395190517610152)
XLA Ops:
  0.0 0.0 copy-start
  0.0 1.0 fusion.11
  1.0 0.9 fusion.16
  1.9 24.6 %all-gather = bf16[16,2,8192]{2,1,0:T(2,128)(2,1)S(1)} all-gather(bf16[1,2,8192]{2,1,0:T(2,128)(2,1)S(1)} %fusion.16), channel_id=1, replica_groups=mesh['groups'=2,'hid'=16] {'hid'}, dimensions={0}, use_global_device_ids=true | all-gather | bytes 557056 | tf_op jit(solution)/shard_map/all_gather | solution.py:45
  26.5 0.2 reshape.119
  26.7 0.0 copy-start.1
  26.7 0.0 copy-start.2
  26.7 5.0 %convolution_convert_fusion = bf16[32,512]{1,0:T(8,128)(2,1)S(1)} fusion(bf16[32,8192]{1,0:T(8,128)(2,1)S(1)} %reshape.119, bf16[8192,512]{1,0:T(8,128)(2,1)} %param.12), kind=kOutput, calls=%fused_computation.7 | convolution fusion | flops 268451840 | bytes 8945664 | tf_op jit(solution)/shard_map/dot_general | solution.py:47
  31.8 0.0 copy-done
  31.8 0.0 copy-start.3
  31.8 0.4 convolution_convert_fusion.1
  32.2 0.0 copy-done.1
  32.2 0.4 convolution_convert_fusion.2
  32.6 0.1 pad_maximum_fusion
  32.7 0.6 reshape.111
  33.3 3.5 %all-to-all-start = ((bf16[16,2,640]{2,1,0:T(2,128)(2,1)}), bf16[16,2,640]{2,1,0:T(2,128)(2,1)S(1)}, u32[]{:S(2)}, u32[]{:S(2)}) async-start(bf16[16,2,640]{2,1,0:T(2,128)(2,1)} %reshape.111), calls=%async_computation | async-start | bytes 81920 | tf_op jit(solution)/shard_map/all_to_all | solution.py:51
  37.5 0.0 copy-done.2
  37.5 0.3 copy.57
  38.5 1.5 %copy.58 = bf16[64,8,8,128]{3,2,1,0:T(8,128)(2,1)S(1)} copy(bf16[64,8,8,128]{3,1,2,0:T(8,128)(2,1)} %bitcast.67) | data formatting | bytes 2097152
  40.0 0.1 multiply_cosine_fusion
  40.1 3.4 %all-to-all-done = bf16[16,2,640]{2,1,0:T(2,128)(2,1)S(1)} async-done(((bf16[16,2,640]{2,1,0:T(2,128)(2,1)}), bf16[16,2,640]{2,1,0:T(2,128)(2,1)S(1)}, u32[]{:S(2)}, u32[]{:S(2)}) %all-to-all-start) | async-done | bytes 40992 | tf_op jit(solution)/shard_map/all_to_all | solution.py:51
  43.5 0.1 fusion.26
  43.6 0.1 reshape.117
  43.7 0.1 fusion.27
  43.8 0.1 fusion.13
  43.9 0.5 fusion.28
  44.4 0.4 fusion.29
  44.8 0.2 fusion.8
  45.0 0.1 reshape.112
  45.1 0.3 convolution_bitcast_fusion.1
  45.4 0.2 fusion.3
  45.7 0.6 copy.43
  46.4 3.5 %all-to-all-start.1 = ((bf16[16,2,512]{2,1,0:T(2,128)(2,1)}), bf16[16,2,512]{2,1,0:T(2,128)(2,1)S(1)}, u32[]{:S(2)}, u32[]{:S(2)}) async-start(bf16[16,2,512]{2,1,0:T(2,128)(2,1)} %copy.43), calls=%async_computation.1 | async-start | bytes 65536 | tf_op jit(solution)/shard_map/all_to_all | solution.py:88
  49.9 0.0 copy-done.3
  49.9 0.7 dynamic-slice
  51.2 5.2 %all-to-all-done.1 = bf16[16,2,512]{2,1,0:T(2,128)(2,1)S(1)} async-done(((bf16[16,2,512]{2,1,0:T(2,128)(2,1)}), bf16[16,2,512]{2,1,0:T(2,128)(2,1)S(1)}, u32[]{:S(2)}, u32[]{:S(2)}) %all-to-all-start.1) | async-done | bytes 32800 | tf_op jit(solution)/shard_map/all_to_all | solution.py:88
  56.5 4.9 %fusion.30 = f32[32,8192]{1,0:T(8,128)S(1)} fusion(bf16[32,512]{1,0:T(8,128)(2,1)S(1)} %reshape.114, bf16[512,8192]{1,0:T(8,128)(2,1)} %param.15), kind=kOutput, calls=%fused_computation.61 | convolution fusion | flops 268435456 | bytes 9469952 | tf_op jit(solution)/shard_map/dot_general | solution.py:89
  61.4 69.3 %all-reduce.2 = bf16[32,8192]{1,0:T(8,128)(2,1)S(1)} all-reduce(f32[32,8192]{1,0:T(8,128)S(1)} %fusion.30), channel_id=2, replica_groups=mesh['groups'=2,'hid'=16] {'hid'}, use_global_device_ids=true, to_apply=%region_5.6.clone | all-reduce | flops 262144 | bytes 1572864
  130.8 0.7 fusion.15
  (15 shorter events, 0.2 us)
Async XLA Ops:
  0.0 31.8 %copy-start = (bf16[8192,64]{0,1:T(8,128)(2,1)S(1)}, bf16[8192,64]{0,1:T(8,128)(2,1)}, u32[]{:S(2)}) copy-start(bf16[8192,64]{0,1:T(8,128)(2,1)} %param.14) | copy-start | bytes 3145732
  26.7 5.5 %copy-start.1 = (bf16[8192,64]{0,1:T(8,128)(2,1)S(1)}, bf16[8192,64]{0,1:T(8,128)(2,1)}, u32[]{:S(2)}) copy-start(bf16[8192,64]{0,1:T(8,128)(2,1)} %param.13) | copy-start | bytes 3145732
  26.7 10.8 %copy-start.2 = (bf16[1,512,1024]{2,1,0:T(8,128)(2,1)S(1)}, bf16[1,512,1024]{2,1,0:T(8,128)(2,1)}, u32[]{:S(2)}) copy-start(bf16[1,512,1024]{2,1,0:T(8,128)(2,1)} %param.16) | copy-start | bytes 3145732
  31.8 18.1 %copy-start.3 = (u32[32]{0:T(128)S(1)}, u32[32]{0:T(128)}, u32[]{:S(2)}) copy-start(u32[32]{0:T(128)} %constant.21) | copy-start | bytes 388
  33.3 10.2 %all-to-all-start = ((bf16[16,2,640]{2,1,0:T(2,128)(2,1)}), bf16[16,2,640]{2,1,0:T(2,128)(2,1)S(1)}, u32[]{:S(2)}, u32[]{:S(2)}) async-start(bf16[16,2,640]{2,1,0:T(2,128)(2,1)} %reshape.111), calls=%async_computation | async-start | bytes 81920 | tf_op jit(solution)/shard_map/all_to_all | solution.py:51
  46.4 10.1 %all-to-all-start.1 = ((bf16[16,2,512]{2,1,0:T(2,128)(2,1)}), bf16[16,2,512]{2,1,0:T(2,128)(2,1)S(1)}, u32[]{:S(2)}, u32[]{:S(2)}) async-start(bf16[16,2,512]{2,1,0:T(2,128)(2,1)} %copy.43), calls=%async_computation.1 | async-start | bytes 65536 | tf_op jit(solution)/shard_map/all_to_all | solution.py:88
where the time goes:
time: 132 us; the launch traced here: 131 us
  blocking collectives  93.9 us (71%)
  matrix products  12.2 us (9%)
  waiting for transfers between devices  8.63 us (7%)
  starting transfers between devices  6.99 us (5%)
  local copies, waits for them, and re-layouts  4.91 us (4%)
  other arithmetic  2.56 us (2%)
  between operations  2.22 us (2%)
    unnamed x1, blocking collectives  69.3 us
    all_gather x1, blocking collectives, per_device(): rows = lax.all_gather(normed, 'hid', axis=0, tiled=True)  24.6 us
    dot_general x3, matrix products, per_device(): jnp.dot(rows, w, preferred_element_type=jnp.float32).astype(jnp.bfloat16)  5.85 us
    all_to_all x1, waiting for transfers between devices, per_device(): lax.all_to_all(mixed, 'hid', split_axis=0, concat_axis=0, tiled=True)  5.22 us
    dot_general x1, matrix products, per_device(): jnp.dot(heads.reshape(size * steps, query_width), w_out, preferred_elemen...  4.92 us
    all_to_all x1, starting transfers between devices, per_device(): lax.all_to_all(mixed, 'hid', split_axis=0, concat_axis=0, tiled=True)  3.5 us
    all_to_all x1, starting transfers between devices, per_device(): lax.all_to_all(columns, 'hid', split_axis=0, concat_axis=0, tiled=True)  3.5 us
    all_to_all x1, waiting for transfers between devices, per_device(): lax.all_to_all(columns, 'hid', split_axis=0, concat_axis=0, tiled=True)  3.41 us
  transfers between devices with their start and end apart: 2, of which 2 were waited for; matrix products, arithmetic and copies ran while one was open for 2% of the time, Pallas kernels for 0%

commit v1 on v0

v1 whole, which is shorter than its diff:
```python
import functools
import math

import jax
import jax.numpy as jnp
from jax import lax
from jax.experimental import pallas as pl
from jax.experimental.pallas import tpu as pltpu
from jax.sharding import PartitionSpec as P

HEADS = 64
KV_HEADS = 8
HEAD = 128
STEPS = 2
CHUNKS = 8
F32 = jnp.float32
BF16 = jnp.bfloat16


def push(src, dst, send, recv, peer):
    return pltpu.make_async_remote_copy(
        src_ref=src,
        dst_ref=dst,
        send_sem=send,
        recv_sem=recv,
        device_id={"hid": peer},
        device_id_type=pl.DeviceIdType.MESH,
    )


def kernel(
    n, positions, lengths, tokens, wq_hbm, wk_hbm, wv_hbm, wo_hbm, ck_hbm, cv_hbm, out,
    wq, wk, wv, wo, ck, cv,
    x_raw, x_land, x_tmp, x_rows,
    y_rows, kv_pad, q_pack, q_send, q_land, q_wide, q_rows, k_rows, v_rows,
    m_send, m_land, a_rows,
    p_rows, p_pack, p_send, p_land, o_rows,
    load_sem, x_ss, x_rs, q_ss, q_rs, m_ss, m_rs, p_ss, p_rs,
):
    me = lax.axis_index("hid")
    wide = x_raw.shape[1]
    query_width = wq.shape[1]
    own_heads = query_width // HEAD
    head_rows = STEPS * own_heads
    key_width = wk.shape[1]
    per = HEAD // key_width
    capacity = ck.shape[0]

    loads = [
        pltpu.make_async_copy(src, dst, load_sem.at[i])
        for i, (src, dst) in enumerate(
            [(wq_hbm, wq), (wk_hbm, wk), (wv_hbm, wv), (ck_hbm.at[0], ck), (cv_hbm.at[0], cv), (wo_hbm, wo)]
        )
    ]
    for load in loads:
        load.start()

    barrier = pltpu.get_barrier_semaphore()

    @pl.loop(1, n)
    def _(k):
        pl.semaphore_signal(
            barrier, inc=1, device_id={"hid": lax.rem(me + k, n)}, device_id_type=pl.DeviceIdType.MESH
        )

    for step in range(STEPS):
        for c in range(CHUNKS):
            x_raw[STEPS * c + step : STEPS * c + step + 1, :] = tokens[
                step, :, c * wide : (c + 1) * wide
            ].astype(F32)
    raw = x_raw[...]
    squares = jnp.sum(raw * raw, axis=1, keepdims=True)
    odd = lax.broadcasted_iota(jnp.int32, squares.shape, 0) % STEPS == 1
    width = CHUNKS * wide
    mean_even = jnp.sum(jnp.where(odd, 0.0, squares), axis=0, keepdims=True) / width
    mean_odd = jnp.sum(jnp.where(odd, squares, 0.0), axis=0, keepdims=True) / width
    factor = lax.rsqrt(jnp.where(odd, mean_odd, mean_even) + 1e-06)
    x_land[me] = (raw * factor).astype(BF16)

    pl.semaphore_wait(barrier, n - 1)

    def send_all(src_of, land, ss, rs):
        @pl.loop(1, n)
        def _(k):
            peer = lax.rem(me + k, n)
            push(src_of(peer), land.at[me], ss.at[peer], rs.at[me], peer).start()

    def wait_from(s, land, ss, rs):
        @pl.when(s != me)
        def _():
            push(land.at[s], land.at[s], ss.at[s], rs.at[s], s).wait_recv()

    def wait_sends(src_of, land, ss, rs):
        @pl.loop(1, n)
        def _(k):
            peer = lax.rem(me + k, n)
            push(src_of(peer), land.at[me], ss.at[peer], rs.at[me], peer).wait_send()

    send_all(lambda peer: x_land.at[me], x_land, x_ss, x_rs)

    tile = (2 * KV_HEADS, HEAD)
    lane = lax.broadcasted_iota(jnp.int32, tile, 1)
    row = lax.broadcasted_iota(jnp.int32, tile, 0)
    place = (positions[0] + row % STEPS).astype(F32)
    inverse = jnp.exp((lane % (HEAD // 2)).astype(F32) * (-2.0 * math.log(1000000.0) / HEAD))
    angle = place * inverse
    cosine = jnp.cos(angle)
    sine = jnp.sin(angle)
    sine = jnp.where(lane < HEAD // 2, -sine, sine)

    def rotate(values):
        return values * cosine + pltpu.roll(values, HEAD // 2, 1) * sine

    kv_pad[...] = jnp.zeros_like(kv_pad)
    q_pack[...] = jnp.zeros_like(q_pack)

    for s in range(n):
        wait_from(s, x_land, x_ss, x_rs)
        x_tmp[s] = x_land[s].astype(F32)
        for c in range(CHUNKS):
            x_rows[c, STEPS * s : STEPS * (s + 1), :] = x_tmp[s, STEPS * c : STEPS * (c + 1), :]

    for load in loads[:3]:
        load.wait()
    rows = STEPS * n

    def project(c, sums):
        left = x_rows[c].astype(BF16)
        part = pl.ds(pl.multiple_of(c * wide, wide), wide)
        return tuple(
            total + jnp.dot(left, w[part, :], preferred_element_type=F32)
            for total, w in zip(sums, (wq, wk, wv))
        )

    query, key, value = lax.fori_loop(
        0,
        CHUNKS,
        project,
        (
            jnp.zeros((rows, query_width), F32),
            jnp.zeros((rows, key_width), F32),
            jnp.zeros((rows, key_width), F32),
        ),
    )
    y_rows[:, :query_width] = query
    shift = lax.rem(me, per) * key_width
    kv_pad[0, :, :key_width] = key
    kv_pad[1, :, :key_width] = value
    y_rows[:, query_width : query_width + HEAD] = pltpu.roll(kv_pad[0], shift, 1)
    y_rows[:, query_width + HEAD :] = pltpu.roll(kv_pad[1], shift, 1)
    for d in range(n):
        for j in range(own_heads + 2):
            q_pack[d, STEPS * j : STEPS * (j + 1), :] = y_rows[
                STEPS * d : STEPS * (d + 1), j * HEAD : (j + 1) * HEAD
            ]
    q_send[...] = q_pack[...].astype(BF16)
    q_land[me] = q_send[me]
    send_all(lambda peer: q_send.at[peer], q_land, q_ss, q_rs)
    wait_sends(lambda peer: x_land.at[me], x_land, x_ss, x_rs)

    k_rows[...] = jnp.zeros_like(k_rows)
    v_rows[...] = jnp.zeros_like(v_rows)
    for s in range(n):
        wait_from(s, q_land, q_ss, q_rs)
        q_wide[s] = q_land[s].astype(F32)
        q_rows[head_rows * s : head_rows * (s + 1), :] = q_wide[s, :head_rows, :]
        g = s // per
        pair = slice(STEPS * g, STEPS * (g + 1))
        k_rows[pair, :] += q_wide[s, head_rows : head_rows + STEPS, :]
        v_rows[pair, :] += q_wide[s, head_rows + STEPS : head_rows + 2 * STEPS, :]
    k_rows[...] = rotate(k_rows[...])

    for load in loads[3:5]:
        load.wait()
    group_rows = STEPS * (HEADS // KV_HEADS)
    position = lax.broadcasted_iota(jnp.int32, (group_rows, capacity), 1)
    query_step = lax.broadcasted_iota(jnp.int32, (group_rows, capacity), 0) % STEPS
    seen = (position < lengths[0]) | (
        (position >= capacity - STEPS) & (position - (capacity - STEPS) <= query_step)
    )
    last = 16
    last_row = lax.broadcasted_iota(jnp.int32, (last, HEAD), 0)
    per_dest = head_rows
    for g in range(KV_HEADS):
        lanes = slice(g * HEAD, (g + 1) * HEAD)
        for cache, fresh in ((ck, k_rows), (cv, v_rows)):
            end = cache[capacity - last : capacity, lanes].astype(F32)
            for step in range(STEPS):
                r = STEPS * g + step
                end = jnp.where(last_row == last - STEPS + step, fresh[r : r + 1, :], end)
            cache[capacity - last : capacity, lanes] = end.astype(BF16)
        q = rotate(q_rows[group_rows * g : group_rows * (g + 1), :]).astype(BF16)
        scores = lax.dot_general(
            q, ck[:, lanes], (((1,), (1,)), ((), ())), preferred_element_type=F32
        ) * (HEAD ** -0.5)
        scores = jnp.where(seen, scores, -jnp.inf)
        grown = jnp.exp(scores - jnp.max(scores, axis=1, keepdims=True))
        weights = (grown / jnp.sum(grown, axis=1, keepdims=True)).astype(BF16)
        mixed = jnp.dot(weights, cv[:, lanes], preferred_element_type=F32)
        q_rows[group_rows * g : group_rows * (g + 1), :] = mixed
    for d in range(n):
        m_send[d, :per_dest, :] = q_rows[per_dest * d : per_dest * (d + 1), :]
    m_land[me] = m_send[me]
    send_all(lambda peer: m_send.at[peer], m_land, m_ss, m_rs)
    wait_sends(lambda peer: q_send.at[peer], q_land, q_ss, q_rs)
    loads[5].wait()

    for s in range(n):
        wait_from(s, m_land, m_ss, m_rs)
        for j in range(own_heads):
            a_rows[STEPS * s : STEPS * (s + 1), j * HEAD : (j + 1) * HEAD] = m_land[
                s, STEPS * j : STEPS * (j + 1), :
            ]
    left = a_rows[...].astype(BF16)

    @pl.loop(0, CHUNKS)
    def _(c):
        part = pl.ds(pl.multiple_of(c * wide, wide), wide)
        p_rows[c] = jnp.dot(left, wo[:, part], preferred_element_type=F32)

    for d in range(n):
        for c in range(CHUNKS):
            p_pack[d, STEPS * c : STEPS * (c + 1), :] = p_rows[c, STEPS * d : STEPS * (d + 1), :]
        p_send[d] = p_pack[d].astype(BF16)
    p_land[me] = p_send[me]
    send_all(lambda peer: p_send.at[peer], p_land, p_ss, p_rs)
    wait_sends(lambda peer: m_send.at[peer], m_land, m_ss, m_rs)

    total = p_pack[me]
    for s in range(n):
        wait_from(s, p_land, p_ss, p_rs)
        total = total + jnp.where(s == me, 0.0, p_land[s].astype(F32))
    o_rows[...] = total
    for step in range(STEPS):
        for c in range(CHUNKS):
            r = STEPS * c + step
            out[step, :, c * wide : (c + 1) * wide] = o_rows[r : r + 1, :].astype(BF16)
    wait_sends(lambda peer: p_send.at[peer], p_land, p_ss, p_rs)


def per_device(
    tokens, positions, lengths, w_query, w_key, w_value, w_out, cache_keys, cache_values
):
    n = lax.axis_size("hid")
    width = tokens.shape[2]
    wide = width // CHUNKS
    packed = STEPS * CHUNKS
    query_width, key_width = w_query.shape[1], w_key.shape[1]
    own_heads = query_width // HEAD
    _, capacity, kv_width = cache_keys.shape
    rows = STEPS * n
    message = -(-STEPS * (own_heads + 2) // 16) * 16
    back = -(-STEPS * own_heads // 8) * 8
    smem = pl.BlockSpec(memory_space=pltpu.SMEM)
    vmem = pl.BlockSpec(memory_space=pltpu.VMEM)
    hbm = pl.BlockSpec(memory_space=pltpu.HBM)
    dma = pltpu.SemaphoreType.DMA
    return pl.pallas_call(
        functools.partial(kernel, n),
        out_shape=jax.ShapeDtypeStruct(tokens.shape, BF16),
        in_specs=[smem, smem, vmem] + [hbm] * 6,
        out_specs=vmem,
        scratch_shapes=[
            pltpu.VMEM(w_query.shape, BF16),
            pltpu.VMEM(w_key.shape, BF16),
            pltpu.VMEM(w_value.shape, BF16),
            pltpu.VMEM(w_out.shape, BF16),
            pltpu.VMEM((capacity, kv_width), BF16),
            pltpu.VMEM((capacity, kv_width), BF16),
            pltpu.VMEM((packed, wide), F32),
            pltpu.VMEM((n, packed, wide), BF16),
            pltpu.VMEM((n, packed, wide), F32),
            pltpu.VMEM((CHUNKS, rows, wide), F32),
            pltpu.VMEM((rows, query_width + 2 * HEAD), F32),
            pltpu.VMEM((2, rows, HEAD), F32),
            pltpu.VMEM((n, message, HEAD), F32),
            pltpu.VMEM((n, message, HEAD), BF16),
            pltpu.VMEM((n, message, HEAD), BF16),
            pltpu.VMEM((n, message, HEAD), F32),
            pltpu.VMEM((STEPS * HEADS, HEAD), F32),
            pltpu.VMEM((STEPS * KV_HEADS, HEAD), F32),
            pltpu.VMEM((STEPS * KV_HEADS, HEAD), F32),
            pltpu.VMEM((n, back, HEAD), F32),
            pltpu.VMEM((n, back, HEAD), F32),
            pltpu.VMEM((rows, query_width), F32),
            pltpu.VMEM((CHUNKS, rows, wide), F32),
            pltpu.VMEM((n, packed, wide), F32),
            pltpu.VMEM((n, packed, wide), BF16),
            pltpu.VMEM((n, packed, wide), BF16),
            pltpu.VMEM((packed, wide), F32),
            dma((6,)),
        ]
        + [dma((n,))] * 8,
        compiler_params=pltpu.CompilerParams(
            collective_id=0, has_side_effects=True, vmem_limit_bytes=56 * 2**20
        ),
    )(positions, lengths, tokens, w_query, w_key, w_value, w_out, cache_keys, cache_values)


def solution(mesh):
    return jax.shard_map(
        per_device,
        mesh=mesh,
        in_specs=(
            P(None, ("groups", "hid"), None),
            P(("groups", "hid")),
            P(("groups", "hid")),
            P(None, "hid"),
            P(None, "hid"),
            P(None, "hid"),
            P("hid", None),
            P(("groups", "hid"), None, None),
            P(("groups", "hid"), None, None),
        ),
        out_specs=P(None, ("groups", "hid"), None),
        check_vma=False,
    )
```

time: 132 us -> 60.2 us (0.46)
  the two profiles are of different devices: /device:TPU:0 before, /device:TPU:9 now
where the time goes in v1:
time: 60.2 us; the launch traced here: 59.8 us
  Pallas kernels  50.1 us (83%)
  local copies, waits for them, and re-layouts  8.45 us (14%)
  between operations  1.31 us (2%)
    pallas_call x1, Pallas kernels, per_device(): pl.pallas_call(functools.partial(kernel, n), out_shape=jax.ShapeDtypeStru...  50.1 us
    unnamed x3, local copies, waits for them, and re-layouts  6.94 us
    pallas_call x1, local copies, waits for them, and re-layouts, per_device(): pl.pallas_call(functools.partial(kernel, n), out_shape=jax.ShapeDtypeStru...  1.51 us

profile of v1, /device:TPU:9, one launch (start us, length us, event | category | flops | bytes accessed | tf_op | source)
XLA Modules:
  0.0 59.8 jit_solution(2409494180273765290)
XLA Ops:
  1.3 1.4 %copy.10.tokens = bf16[2,1,8192]{2,1,0:T(2,128)(2,1)} copy(bf16[2,1,8192]{2,0,1:T(2,128)(2,1)} %param.9) | data formatting | bytes 65536 | tf_op args[0]
  2.7 2.8 %copy.11.wk_hbm = bf16[8192,64]{1,0:T(8,128)(2,1)} copy(bf16[8192,64]{0,1:T(8,128)(2,1)} %param.13) | data formatting | bytes 2097152 | tf_op args[4]
  5.5 2.7 %copy.12.wv_hbm = bf16[8192,64]{1,0:T(8,128)(2,1)} copy(bf16[8192,64]{0,1:T(8,128)(2,1)} %param.14) | data formatting | bytes 2097152 | tf_op args[5]
  8.2 50.1 %shard_map.91 = bf16[2,1,8192]{2,1,0:T(2,128)(2,1)} custom-call(s32[1]{0:T(128)S(6)} %copy.14.positions, s32[1]{0:T(128)S(6)} %copy.15.lengths, bf16[2,1,8192]{2,1,0:T(2,128)(2,1)} %copy.10.tokens, bf16[8192,512]{1,0:T(8,128)(2,1)} %wq_hbm.1, bf16[8192,64]{1,0:T(8,128)(2,1)} %copy.11.wk_hbm, bf16[8192,64]{1,0:T(8,128)(2,1)} %copy.12.wv_hbm, ...), custom_call_target="tpu_custom_call" | custom-call | tf_op jit(solution)/shard_map/pallas_call | solution.py:258
  58.3 1.5 %copy.13 = bf16[2,1,8192]{2,0,1:T(2,128)(2,1)} copy(bf16[2,1,8192]{2,1,0:T(2,128)(2,1)} %shard_map.91) | data formatting | bytes 65536 | tf_op jit(solution)/shard_map/pallas_call | solution.py:258

commit v2 on v1

v2 whole, which is shorter than its diff:
```python
import functools
import math

import jax
import jax.numpy as jnp
from jax import lax
from jax.experimental import pallas as pl
from jax.experimental.pallas import tpu as pltpu
from jax.sharding import PartitionSpec as P

HEADS = 64
KV_HEADS = 8
HEAD = 128
STEPS = 2
CHUNKS = 8
F32 = jnp.float32
BF16 = jnp.bfloat16


def push(src, dst, send, recv, peer):
    return pltpu.make_async_remote_copy(
        src_ref=src,
        dst_ref=dst,
        send_sem=send,
        recv_sem=recv,
        device_id={"hid": peer},
        device_id_type=pl.DeviceIdType.MESH,
    )


def kernel(
    n, positions, lengths, tokens, wq_hbm, wk_hbm, wv_hbm, wo_hbm, ck_hbm, cv_hbm, out,
    wq, wkv, wo, ck, cv,
    x_raw, x_land, x_tmp, x_rows,
    y_rows, kv_pad, q_pack, q_send, q_land, q_wide, q_rows, k_rows, v_rows,
    m_send, m_land, a_rows,
    p_rows, h_send, h_land, p_pack, p_send, p_land, o_rows,
    load_sem, x_ss, x_rs, q_ss, q_rs, m_ss, m_rs, h_ss, h_rs, p_ss, p_rs,
):
    me = lax.axis_index("hid")
    chips = n // 2
    chip, core = me // 2, lax.rem(me, 2)
    partner = chip * 2 + (1 - core)
    wide = x_raw.shape[1]
    query_width = wq.shape[1]
    own_heads = query_width // HEAD
    head_rows = STEPS * own_heads
    key_width = wkv.shape[0] // 2
    per = HEAD // key_width
    capacity = ck.shape[0]
    rows = STEPS * n
    half = rows // 2

    def device(i):
        other = i // chips
        return lax.rem(chip + i % chips, chips) * 2 + lax.rem(core + other, 2)

    loads = [
        pltpu.make_async_copy(src, dst, load_sem.at[i])
        for i, (src, dst) in enumerate(
            [
                (wq_hbm, wq),
                (wk_hbm, wkv.at[:key_width]),
                (wv_hbm, wkv.at[key_width:]),
                (ck_hbm.at[0], ck),
                (cv_hbm.at[0], cv),
                (wo_hbm, wo),
            ]
        )
    ]
    for load in loads:
        load.start()

    barrier = pltpu.get_barrier_semaphore()

    @pl.loop(1, n)
    def _(k):
        pl.semaphore_signal(
            barrier, inc=1, device_id={"hid": lax.rem(me + k, n)}, device_id_type=pl.DeviceIdType.MESH
        )

    for c in range(CHUNKS):
        x_raw[STEPS * c : STEPS * (c + 1), :] = tokens[:, c * wide : (c + 1) * wide].astype(F32)
    raw = x_raw[...]
    squares = jnp.sum(raw * raw, axis=1, keepdims=True)
    odd = lax.broadcasted_iota(jnp.int32, squares.shape, 0) % STEPS == 1
    width = CHUNKS * wide
    mean_even = jnp.sum(jnp.where(odd, 0.0, squares), axis=0, keepdims=True) / width
    mean_odd = jnp.sum(jnp.where(odd, squares, 0.0), axis=0, keepdims=True) / width
    factor = lax.rsqrt(jnp.where(odd, mean_odd, mean_even) + 1e-06)
    x_land[me] = (raw * factor).astype(BF16)

    pl.semaphore_wait(barrier, n - 1)

    def wait_recv(s, land, ss, rs):
        push(land.at[s], land.at[s], ss.at[s], rs.at[s], s).wait_recv()

    def exchange(i, src, land, ss, rs):
        peer = device(i)
        return push(src, land.at[me], ss.at[peer], rs.at[me], peer)

    def direct(peer):
        return push(x_land.at[me], x_land.at[me], x_ss.at[peer], x_rs.at[me], peer)

    def forward(s, spare):
        return push(x_land.at[s], x_land.at[s], x_ss.at[spare], x_rs.at[s], partner)

    for kc in range(1, chips):
        direct(device(kc)).start()
    direct(partner).start()

    tile = (2 * KV_HEADS, HEAD)
    lane = lax.broadcasted_iota(jnp.int32, tile, 1)
    row = lax.broadcasted_iota(jnp.int32, tile, 0)
    place = (positions[0] + row % STEPS).astype(F32)
    inverse = jnp.exp((lane % (HEAD // 2)).astype(F32) * (-2.0 * math.log(1000000.0) / HEAD))
    angle = place * inverse
    cosine = jnp.cos(angle)
    sine = jnp.sin(angle)
    sine = jnp.where(lane < HEAD // 2, -sine, sine)

    def rotate(values):
        return values * cosine + pltpu.roll(values, HEAD // 2, 1) * sine

    kv_pad[...] = jnp.zeros_like(kv_pad)
    q_pack[...] = jnp.zeros_like(q_pack)

    def unpack(i):
        x_tmp[i] = x_land[device(i)].astype(F32)
        for c in range(CHUNKS):
            x_rows[c, STEPS * i : STEPS * (i + 1), :] = x_tmp[i, STEPS * c : STEPS * (c + 1), :]

    unpack(0)
    for kc in range(chips - 1, 0, -1):
        s = device(kc)
        wait_recv(s, x_land, x_ss, x_rs)
        forward(s, device(kc + chips)).start()
        unpack(kc)
    for kc in [0] + list(range(chips - 1, 0, -1)):
        wait_recv(device(kc + chips), x_land, x_ss, x_rs)
        unpack(kc + chips)

    for load in loads[:3]:
        load.wait()

    def project(c, sums):
        left = x_rows[c].astype(BF16)
        part = pl.ds(pl.multiple_of(c * wide, wide), wide)
        query = sums[0] + jnp.dot(left, wq[part, :], preferred_element_type=F32)
        fresh = sums[1] + lax.dot_general(
            left, wkv[:, part], (((1,), (1,)), ((), ())), preferred_element_type=F32
        )
        return query, fresh

    query, fresh = lax.fori_loop(
        0,
        CHUNKS,
        project,
        (jnp.zeros((rows, query_width), F32), jnp.zeros((rows, 2 * key_width), F32)),
    )
    y_rows[:, :query_width] = query
    kv_pad[:, : 2 * key_width] = fresh
    spot = lax.rem(me, per)
    both = kv_pad[...]
    here = lax.broadcasted_iota(jnp.int32, both.shape, 1) // key_width == spot
    key = pltpu.roll(both, spot * key_width, 1)
    value = pltpu.roll(both, lax.rem(spot + per - 1, per) * key_width, 1)
    y_rows[:, query_width : query_width + HEAD] = jnp.where(here, key, 0.0)
    y_rows[:, query_width + HEAD :] = jnp.where(here, value, 0.0)
    for i in range(n):
        for j in range(own_heads + 2):
            q_pack[i, STEPS * j : STEPS * (j + 1), :] = y_rows[
                STEPS * i : STEPS * (i + 1), j * HEAD : (j + 1) * HEAD
            ]
    q_send[...] = q_pack[...].astype(BF16)
    for i in range(1, n):
        exchange(i, q_send.at[i], q_land, q_ss, q_rs).start()
    q_land[me] = q_send[0]
    for kc in range(1, chips):
        direct(device(kc)).wait_send()
        forward(device(kc), device(kc + chips)).wait_send()
    direct(partner).wait_send()

    k_rows[...] = jnp.zeros_like(k_rows)
    v_rows[...] = jnp.zeros_like(v_rows)
    for load in loads[3:5]:
        load.wait()
    for i in range(1, n):
        wait_recv(device(i), q_land, q_ss, q_rs)
    for s in range(n):
        q_wide[s] = q_land[s].astype(F32)
        q_rows[head_rows * s : head_rows * (s + 1), :] = q_wide[s, :head_rows, :]
        g = s // per
        pair = slice(STEPS * g, STEPS * (g + 1))
        k_rows[pair, :] += q_wide[s, head_rows : head_rows + STEPS, :]
        v_rows[pair, :] += q_wide[s, head_rows + STEPS : head_rows + 2 * STEPS, :]
    k_rows[...] = rotate(k_rows[...])

    group_rows = STEPS * (HEADS // KV_HEADS)
    position = lax.broadcasted_iota(jnp.int32, (group_rows, capacity), 1)
    query_step = lax.broadcasted_iota(jnp.int32, (group_rows, capacity), 0) % STEPS
    seen = (position < lengths[0]) | (
        (position >= capacity - STEPS) & (position - (capacity - STEPS) <= query_step)
    )
    last = 16
    last_row = lax.broadcasted_iota(jnp.int32, (last, HEAD), 0)
    heads = [slice(g * HEAD, (g + 1) * HEAD) for g in range(KV_HEADS)]
    groups = [slice(g * group_rows, (g + 1) * group_rows) for g in range(KV_HEADS)]
    for g, lanes in enumerate(heads):
        for cache, new in ((ck, k_rows), (cv, v_rows)):
            end = cache[capacity - last : capacity, lanes].astype(F32)
            for step in range(STEPS):
                r = STEPS * g + step
                end = jnp.where(last_row == last - STEPS + step, new[r : r + 1, :], end)
            cache[capacity - last : capacity, lanes] = end.astype(BF16)
    turned = [rotate(q_rows[group, :]).astype(BF16) for group in groups]
    scores = [
        lax.dot_general(
            q, ck[:, lanes], (((1,), (1,)), ((), ())), preferred_element_type=F32
        )
        for q, lanes in zip(turned, heads)
    ]
    scores = [jnp.where(seen, score * (HEAD ** -0.5), -jnp.inf) for score in scores]
    highest = [jnp.max(score, axis=1, keepdims=True) for score in scores]
    grown = [jnp.exp(score - high) for score, high in zip(scores, highest)]
    totals = [jnp.sum(part, axis=1, keepdims=True) for part in grown]
    weights = [(part / total).astype(BF16) for part, total in zip(grown, totals)]
    mixed = [
        jnp.dot(weight, cv[:, lanes], preferred_element_type=F32)
        for weight, lanes in zip(weights, heads)
    ]
    per_group = n // KV_HEADS
    for g in range(KV_HEADS):
        for t in range(per_group):
            m_send[g * per_group + t, :head_rows, :] = mixed[g][
                head_rows * t : head_rows * (t + 1), :
            ]
    for i in range(1, n):
        exchange(i, m_send.at[device(i)], m_land, m_ss, m_rs).start()
    m_land[me] = m_send[me]
    for i in range(1, n):
        exchange(i, q_send.at[i], q_land, q_ss, q_rs).wait_send()
    loads[5].wait()

    for i in [0] + list(range(n - 1, 0, -1)):
        s = device(i)
        if i:
            wait_recv(s, m_land, m_ss, m_rs)
    for s in range(n):
        for j in range(own_heads):
            a_rows[s * STEPS : (s + 1) * STEPS, j * HEAD : (j + 1) * HEAD] = m_land[
                device(s), STEPS * j : STEPS * (j + 1), :
            ]
    left = a_rows[...].astype(BF16)

    def halve(c):
        return push(h_send.at[c], h_land.at[c], h_ss.at[c], h_rs.at[c], partner)

    for c in range(CHUNKS):
        part = jnp.dot(left, wo[:, c * wide : (c + 1) * wide], preferred_element_type=F32)
        h_send[c] = part[half:, :].astype(BF16)
        halve(c).start()
        p_rows[c] = part[:half, :]
    for c in range(CHUNKS):
        halve(c).wait_recv()
        p_rows[c] = p_rows[c] + h_land[c].astype(F32)
        for kc in range(chips):
            p_pack[kc, STEPS * c : STEPS * (c + 1), :] = p_rows[c, STEPS * kc : STEPS * (kc + 1), :]

    def reduce(kc):
        peer = device(kc)
        return push(p_send.at[kc], p_land.at[chip], p_ss.at[kc], p_rs.at[chip], peer)

    for kc in range(1, chips):
        p_send[kc] = p_pack[kc].astype(BF16)
        reduce(kc).start()
    for i in range(1, n):
        exchange(i, m_send.at[device(i)], m_land, m_ss, m_rs).wait_send()

    o_rows[...] = p_pack[0]
    for kc in range(chips - 1, 0, -1):
        s = lax.rem(chip + kc, chips)
        push(p_land.at[s], p_land.at[s], p_ss.at[kc], p_rs.at[s], device(kc)).wait_recv()
        o_rows[...] += p_land[s].astype(F32)
    for c in range(CHUNKS):
        out[:, c * wide : (c + 1) * wide] = o_rows[STEPS * c : STEPS * (c + 1), :].astype(BF16)
    for c in range(CHUNKS):
        halve(c).wait_send()
    for kc in range(1, chips):
        reduce(kc).wait_send()


def per_device(
    tokens, positions, lengths, w_query, w_key, w_value, w_out, cache_keys, cache_values
):
    n = lax.axis_size("hid")
    width = tokens.shape[2]
    wide = width // CHUNKS
    packed = STEPS * CHUNKS
    query_width, key_width = w_query.shape[1], w_key.shape[1]
    own_heads = query_width // HEAD
    _, capacity, kv_width = cache_keys.shape
    rows = STEPS * n
    message = -(-STEPS * (own_heads + 2) // 16) * 16
    back = -(-STEPS * own_heads // 8) * 8
    smem = pl.BlockSpec(memory_space=pltpu.SMEM)
    vmem = pl.BlockSpec(memory_space=pltpu.VMEM)
    hbm = pl.BlockSpec(memory_space=pltpu.HBM)
    dma = pltpu.SemaphoreType.DMA
    chips = n // 2
    result = pl.pallas_call(
        functools.partial(kernel, n),
        out_shape=jax.ShapeDtypeStruct((STEPS, width), BF16),
        in_specs=[smem, smem, vmem] + [hbm] * 6,
        out_specs=vmem,
        scratch_shapes=[
            pltpu.VMEM(w_query.shape, BF16),
            pltpu.VMEM((2 * key_width, width), BF16),
            pltpu.VMEM(w_out.shape, BF16),
            pltpu.VMEM((capacity, kv_width), BF16),
            pltpu.VMEM((capacity, kv_width), BF16),
            pltpu.VMEM((packed, wide), F32),
            pltpu.VMEM((n, packed, wide), BF16),
            pltpu.VMEM((n, packed, wide), F32),
            pltpu.VMEM((CHUNKS, rows, wide), F32),
            pltpu.VMEM((rows, query_width + 2 * HEAD), F32),
            pltpu.VMEM((rows, HEAD), F32),
            pltpu.VMEM((n, message, HEAD), F32),
            pltpu.VMEM((n, message, HEAD), BF16),
            pltpu.VMEM((n, message, HEAD), BF16),
            pltpu.VMEM((n, message, HEAD), F32),
            pltpu.VMEM((STEPS * HEADS, HEAD), F32),
            pltpu.VMEM((STEPS * KV_HEADS, HEAD), F32),
            pltpu.VMEM((STEPS * KV_HEADS, HEAD), F32),
            pltpu.VMEM((n, back, HEAD), F32),
            pltpu.VMEM((n, back, HEAD), F32),
            pltpu.VMEM((rows, query_width), F32),
            pltpu.VMEM((CHUNKS, rows // 2, wide), F32),
            pltpu.VMEM((CHUNKS, rows // 2, wide), BF16),
            pltpu.VMEM((CHUNKS, rows // 2, wide), BF16),
            pltpu.VMEM((chips, packed, wide), F32),
            pltpu.VMEM((chips, packed, wide), BF16),
            pltpu.VMEM((chips, packed, wide), BF16),
            pltpu.VMEM((packed, wide), F32),
            dma((6,)),
        ]
        + [dma((n,))] * 6
        + [dma((CHUNKS,))] * 2
        + [dma((chips,))] * 2,
        compiler_params=pltpu.CompilerParams(
            collective_id=0, has_side_effects=True, vmem_limit_bytes=56 * 2**20
        ),
    )(
        positions,
        lengths,
        tokens.reshape(STEPS, width),
        w_query,
        w_key.T,
        w_value.T,
        w_out,
        cache_keys,
        cache_values,
    )
    return result.reshape(tokens.shape)


def solution(mesh):
    return jax.shard_map(
        per_device,
        mesh=mesh,
        in_specs=(
            P(None, ("groups", "hid"), None),
            P(("groups", "hid")),
            P(("groups", "hid")),
            P(None, "hid"),
            P(None, "hid"),
            P(None, "hid"),
            P("hid", None),
            P(("groups", "hid"), None, None),
            P(("groups", "hid"), None, None),
        ),
        out_specs=P(None, ("groups", "hid"), None),
        check_vma=False,
    )
```

time: 60.2 us -> 41.5 us (0.69)
  the two profiles are of different devices: /device:TPU:9 before, /device:TPU:10 now
where the time goes in v2:
time: 41.5 us; the launch traced here: 41.2 us
  Pallas kernels  38.5 us (93%)
  local copies, waits for them, and re-layouts  1.4 us (3%)
  between operations  1.3 us (3%)
    pallas_call x1, Pallas kernels, per_device(): pl.pallas_call(functools.partial(kernel, n), out_shape=jax.ShapeDtypeStru...  38.5 us
    unnamed x1, local copies, waits for them, and re-layouts  1.4 us

profile of v2, /device:TPU:10, one launch (start us, length us, event | category | flops | bytes accessed | tf_op | source)
XLA Modules:
  0.0 41.2 jit_solution(4764101032511738227)
XLA Ops:
  1.3 38.5 %shard_map.91 = bf16[2,8192]{1,0:T(2,128)(2,1)} custom-call(s32[1]{0:T(128)S(6)} %copy.11.positions, s32[1]{0:T(128)S(6)} %copy.12.lengths, bf16[2,8192]{1,0:T(2,128)(2,1)} %bitcast.7, bf16[8192,512]{1,0:T(8,128)(2,1)} %wq_hbm.1, bf16[64,8192]{1,0:T(8,128)(2,1)} %bitcast.4, bf16[64,8192]{1,0:T(8,128)(2,1)} %bitcast.5, bf16[512,8192]{1,0:T(8,128)(2,1)} %wo_hbm.1, ...), custom_call_target="tpu_custom_call" | custom-call | tf_op jit(solution)/shard_map/pallas_call | solution.py:311
  39.9 1.4 %copy.13 = bf16[2,1,8192]{2,0,1:T(2,128)(2,1)} copy(bf16[2,1,8192]{2,0,1:T(2,128)(2,1)} %bitcast.6) | data formatting | bytes 65536

commit v3 on v2

--- a/solution.py
+++ b/solution.py
@@ -51,10 +51,6 @@
     rows = STEPS * n
     half = rows // 2
 
-    def device(i):
-        other = i // chips
-        return lax.rem(chip + i % chips, chips) * 2 + lax.rem(core + other, 2)
-
     loads = [
         pltpu.make_async_copy(src, dst, load_sem.at[i])
         for i, (src, dst) in enumerate(
@@ -105,8 +101,24 @@
     def forward(s, spare):
         return push(x_land.at[s], x_land.at[s], x_ss.at[spare], x_rs.at[s], partner)
 
-    for kc in range(1, chips):
-        direct(device(kc)).start()
+    half_chips = chips // 2
+    side = lax.rem(chip, 2)
+    deck = chip // 2
+
+    def line(k, other):
+        chip_at = lax.rem(deck + k, half_chips) * 2 + lax.rem(side + other, 2)
+        return chip_at * 2 + core
+
+    def across(k):
+        s = line(k, 0)
+        return push(x_land.at[s], x_land.at[s], x_ss.at[line(k, 1)], x_rs.at[s], line(0, 1))
+
+    def mirror(s):
+        return s + 1 - 2 * core
+
+    for k in range(1, half_chips):
+        direct(line(k, 0)).start()
+    across(0).start()
     direct(partner).start()
 
     tile = (2 * KV_HEADS, HEAD)
@@ -125,20 +137,34 @@
     kv_pad[...] = jnp.zeros_like(kv_pad)
     q_pack[...] = jnp.zeros_like(q_pack)
 
+    def device(i):
+        return line(i % half_chips, i // half_chips % 2) + i // chips * (1 - 2 * core)
+
     def unpack(i):
         x_tmp[i] = x_land[device(i)].astype(F32)
         for c in range(CHUNKS):
             x_rows[c, STEPS * i : STEPS * (i + 1), :] = x_tmp[i, STEPS * c : STEPS * (c + 1), :]
 
+    order = [0] + list(range(half_chips - 1, 0, -1))
+    for k in order[1:]:
+        s = line(k, 0)
+        wait_recv(s, x_land, x_ss, x_rs)
+        across(k).start()
+        forward(s, mirror(s)).start()
     unpack(0)
-    for kc in range(chips - 1, 0, -1):
-        s = device(kc)
+    for k in order:
+        s = line(k, 1)
         wait_recv(s, x_land, x_ss, x_rs)
-        forward(s, device(kc + chips)).start()
-        unpack(kc)
-    for kc in [0] + list(range(chips - 1, 0, -1)):
-        wait_recv(device(kc + chips), x_land, x_ss, x_rs)
-        unpack(kc + chips)
+        forward(s, mirror(s)).start()
+        if k:
+            unpack(k)
+    for k in order:
+        unpack(half_chips + k)
+    for k in order:
+        for other in range(2):
+            i = chips + other * half_chips + k
+            wait_recv(device(i), x_land, x_ss, x_rs)
+            unpack(i)
 
     for load in loads[:3]:
         load.wait()
@@ -176,9 +202,12 @@
     for i in range(1, n):
         exchange(i, q_send.at[i], q_land, q_ss, q_rs).start()
     q_land[me] = q_send[0]
-    for kc in range(1, chips):
-        direct(device(kc)).wait_send()
-        forward(device(kc), device(kc + chips)).wait_send()
+    for k in range(half_chips):
+        across(k).wait_send()
+        if k:
+            direct(line(k, 0)).wait_send()
+            forward(line(k, 0), mirror(line(k, 0))).wait_send()
+        forward(line(k, 1), mirror(line(k, 1))).wait_send()
     direct(partner).wait_send()
 
     k_rows[...] = jnp.zeros_like(k_rows)
@@ -279,7 +308,7 @@
 
     o_rows[...] = p_pack[0]
     for kc in range(chips - 1, 0, -1):
-        s = lax.rem(chip + kc, chips)
+        s = device(kc) // 2
         push(p_land.at[s], p_land.at[s], p_ss.at[kc], p_rs.at[s], device(kc)).wait_recv()
         o_rows[...] += p_land[s].astype(F32)
     for c in range(CHUNKS):

time: 41.5 us -> 44 us (1.060)
  the two profiles are of different devices: /device:TPU:10 before, /device:TPU:0 now
where the time goes in v3:
time: 44 us; the launch traced here: 43.7 us
  Pallas kernels  41 us (93%)
  local copies, waits for them, and re-layouts  1.4 us (3%)
  between operations  1.3 us (3%)
    pallas_call x1, Pallas kernels, per_device(): pl.pallas_call(functools.partial(kernel, n), out_shape=jax.ShapeDtypeStru...  41 us
    unnamed x1, local copies, waits for them, and re-layouts  1.4 us

profile of v3, /device:TPU:0, one launch (start us, length us, event | category | flops | bytes accessed | tf_op | source)
XLA Modules:
  0.0 43.7 jit_solution(13775742216520906637)
XLA Ops:
  1.3 41.0 %shard_map.91 = bf16[2,8192]{1,0:T(2,128)(2,1)} custom-call(s32[1]{0:T(128)S(6)} %copy.11.positions, s32[1]{0:T(128)S(6)} %copy.12.lengths, bf16[2,8192]{1,0:T(2,128)(2,1)} %bitcast.7, bf16[8192,512]{1,0:T(8,128)(2,1)} %wq_hbm.1, bf16[64,8192]{1,0:T(8,128)(2,1)} %bitcast.4, bf16[64,8192]{1,0:T(8,128)(2,1)} %bitcast.5, bf16[512,8192]{1,0:T(8,128)(2,1)} %wo_hbm.1, ...), custom_call_target="tpu_custom_call" | custom-call | tf_op jit(solution)/shard_map/pallas_call | solution.py:340
  42.3 1.4 %copy.13 = bf16[2,1,8192]{2,0,1:T(2,128)(2,1)} copy(bf16[2,1,8192]{2,0,1:T(2,128)(2,1)} %bitcast.6) | data formatting | bytes 65536

commit v4 on v2

--- a/solution.py
+++ b/solution.py
@@ -29,8 +29,8 @@
 
 
 def kernel(
-    n, positions, lengths, tokens, wq_hbm, wk_hbm, wv_hbm, wo_hbm, ck_hbm, cv_hbm, out,
-    wq, wkv, wo, ck, cv,
+    n, positions, lengths, tokens_hbm, wq_hbm, wk_hbm, wv_hbm, wo_hbm, ck_hbm, cv_hbm, out,
+    tokens, wq, wkv, wo, ck, cv,
     x_raw, x_land, x_tmp, x_rows,
     y_rows, kv_pad, q_pack, q_send, q_land, q_wide, q_rows, k_rows, v_rows,
     m_send, m_land, a_rows,
@@ -65,12 +65,11 @@
                 (ck_hbm.at[0], ck),
                 (cv_hbm.at[0], cv),
                 (wo_hbm, wo),
+                (tokens_hbm, tokens),
             ]
         )
     ]
-    for load in loads:
-        load.start()
-
+    loads[6].start()
     barrier = pltpu.get_barrier_semaphore()
 
     @pl.loop(1, n)
@@ -78,6 +77,10 @@
         pl.semaphore_signal(
             barrier, inc=1, device_id={"hid": lax.rem(me + k, n)}, device_id_type=pl.DeviceIdType.MESH
         )
+
+    for load in loads[:6]:
+        load.start()
+    loads[6].wait()
 
     for c in range(CHUNKS):
         x_raw[STEPS * c : STEPS * (c + 1), :] = tokens[:, c * wide : (c + 1) * wide].astype(F32)
@@ -310,10 +313,11 @@
     chips = n // 2
     result = pl.pallas_call(
         functools.partial(kernel, n),
-        out_shape=jax.ShapeDtypeStruct((STEPS, width), BF16),
-        in_specs=[smem, smem, vmem] + [hbm] * 6,
+        out_shape=pltpu.VMEM((STEPS, width), BF16),
+        in_specs=[smem, smem] + [hbm] * 7,
         out_specs=vmem,
         scratch_shapes=[
+            pltpu.VMEM((STEPS, width), BF16),
             pltpu.VMEM(w_query.shape, BF16),
             pltpu.VMEM((2 * key_width, width), BF16),
             pltpu.VMEM(w_out.shape, BF16),
@@ -342,7 +346,7 @@
             pltpu.VMEM((chips, packed, wide), BF16),
             pltpu.VMEM((chips, packed, wide), BF16),
             pltpu.VMEM((packed, wide), F32),
-            dma((6,)),
+            dma((7,)),
         ]
         + [dma((n,))] * 6
         + [dma((CHUNKS,))] * 2

time: 41.5 us -> 39.4 us (0.949)
  the two profiles are of different devices: /device:TPU:10 before, /device:TPU:0 now
where the time goes in v4:
time: 39.4 us; the launch traced here: 38.6 us
  Pallas kernels  36.7 us (93%)
  between operations  1.3 us (3%)
  local copies, waits for them, and re-layouts  0.62 us (2%)
    pallas_call x1, Pallas kernels, per_device(): pl.pallas_call(functools.partial(kernel, n), out_shape=pltpu.VMEM((STEPS,...  36.7 us

profile of v4, /device:TPU:0, one launch (start us, length us, event | category | flops | bytes accessed | tf_op | source)
XLA Modules:
  0.0 38.6 jit_solution(18400607074987227372)
XLA Ops:
  1.3 36.7 %shard_map.91 = bf16[2,8192]{1,0:T(2,128)(2,1)S(1)} custom-call(s32[1]{0:T(128)S(6)} %copy.12.positions, s32[1]{0:T(128)S(6)} %copy.13.lengths, bf16[2,8192]{1,0:T(2,128)(2,1)} %bitcast.7, bf16[8192,512]{1,0:T(8,128)(2,1)} %wq_hbm.1, bf16[64,8192]{1,0:T(8,128)(2,1)} %bitcast.5, bf16[64,8192]{1,0:T(8,128)(2,1)} %bitcast.6, bf16[512,8192]{1,0:T(8,128)(2,1)} %wo_hbm.1, ...), custom_call_target="tpu_custom_call" | custom-call | tf_op jit(solution)/shard_map/pallas_call | solution.py:314
  38.0 0.6 %copy.11 = bf16[2,1,8192]{2,0,1:T(2,128)(2,1)} copy(bf16[2,1,8192]{2,0,1:T(2,128)(2,1)S(1)} %bitcast.4) | data formatting | bytes 65536

commit v5 on v4

--- a/solution.py
+++ b/solution.py
@@ -264,33 +264,48 @@
         h_send[c] = part[half:, :].astype(BF16)
         halve(c).start()
         p_rows[c] = part[:half, :]
-    for c in range(CHUNKS):
-        halve(c).wait_recv()
-        p_rows[c] = p_rows[c] + h_land[c].astype(F32)
-        for kc in range(chips):
-            p_pack[kc, STEPS * c : STEPS * (c + 1), :] = p_rows[c, STEPS * kc : STEPS * (kc + 1), :]
-
-    def reduce(kc):
+    slim = wide // 2
+    per_part = CHUNKS // 2
+
+    def reduce(h, kc):
         peer = device(kc)
-        return push(p_send.at[kc], p_land.at[chip], p_ss.at[kc], p_rs.at[chip], peer)
-
-    for kc in range(1, chips):
-        p_send[kc] = p_pack[kc].astype(BF16)
-        reduce(kc).start()
+        to, at = h * chips + kc, h * chips + chip
+        return push(p_send.at[h, kc], p_land.at[h, chip], p_ss.at[to], p_rs.at[at], peer)
+
+    for h in range(2):
+        for c in range(h * per_part, (h + 1) * per_part):
+            halve(c).wait_recv()
+            p_rows[c] = p_rows[c] + h_land[c].astype(F32)
+            for t in range(2):
+                r = STEPS * (2 * (c - h * per_part) + t)
+                for kc in range(chips):
+                    p_pack[h, kc, r : r + STEPS, :] = p_rows[
+                        c, STEPS * kc : STEPS * (kc + 1), t * slim : (t + 1) * slim
+                    ]
+        for kc in range(1, chips):
+            p_send[h, kc] = p_pack[h, kc].astype(BF16)
+            reduce(h, kc).start()
     for i in range(1, n):
         exchange(i, m_send.at[device(i)], m_land, m_ss, m_rs).wait_send()
 
-    o_rows[...] = p_pack[0]
-    for kc in range(chips - 1, 0, -1):
-        s = lax.rem(chip + kc, chips)
-        push(p_land.at[s], p_land.at[s], p_ss.at[kc], p_rs.at[s], device(kc)).wait_recv()
-        o_rows[...] += p_land[s].astype(F32)
-    for c in range(CHUNKS):
-        out[:, c * wide : (c + 1) * wide] = o_rows[STEPS * c : STEPS * (c + 1), :].astype(BF16)
+    for h in range(2):
+        total = p_pack[h, 0]
+        for kc in range(chips - 1, 0, -1):
+            s = lax.rem(chip + kc, chips)
+            to, at = h * chips + kc, h * chips + s
+            push(
+                p_land.at[h, s], p_land.at[h, s], p_ss.at[to], p_rs.at[at], device(kc)
+            ).wait_recv()
+            total = total + p_land[h, s].astype(F32)
+        o_rows[h] = total
+        for c in range(CHUNKS):
+            first = (h * CHUNKS + c) * slim
+            out[:, first : first + slim] = o_rows[h, STEPS * c : STEPS * (c + 1), :].astype(BF16)
     for c in range(CHUNKS):
         halve(c).wait_send()
-    for kc in range(1, chips):
-        reduce(kc).wait_send()
+    for h in range(2):
+        for kc in range(1, chips):
+            reduce(h, kc).wait_send()
 
 
 def per_device(
@@ -342,15 +357,15 @@
             pltpu.VMEM((CHUNKS, rows // 2, wide), F32),
             pltpu.VMEM((CHUNKS, rows // 2, wide), BF16),
             pltpu.VMEM((CHUNKS, rows // 2, wide), BF16),
-            pltpu.VMEM((chips, packed, wide), F32),
-            pltpu.VMEM((chips, packed, wide), BF16),
-            pltpu.VMEM((chips, packed, wide), BF16),
-            pltpu.VMEM((packed, wide), F32),
+            pltpu.VMEM((2, chips, packed, wide // 2), F32),
+            pltpu.VMEM((2, chips, packed, wide // 2), BF16),
+            pltpu.VMEM((2, chips, packed, wide // 2), BF16),
+            pltpu.VMEM((2, packed, wide // 2), F32),
             dma((7,)),
         ]
         + [dma((n,))] * 6
         + [dma((CHUNKS,))] * 2
-        + [dma((chips,))] * 2,
+        + [dma((2 * chips,))] * 2,
         compiler_params=pltpu.CompilerParams(
             collective_id=0, has_side_effects=True, vmem_limit_bytes=56 * 2**20
         ),

time: 39.4 us -> 40.8 us (1.036); the launches traced: 38.6 us -> 40.6 us
  Pallas kernels: 36.7 us -> 38.7 us
    pallas_call x1, Pallas kernels: 36.7 us -> 38.7 us  [per_device(): pl.pallas_call(functools.partial(kernel, n), out_shape=pltpu.VMEM((STEPS,...]
where the time goes in v5:
time: 40.8 us; the launch traced here: 40.6 us
  Pallas kernels  38.7 us (95%)
  between operations  1.3 us (3%)
  local copies, waits for them, and re-layouts  0.62 us (2%)
    pallas_call x1, Pallas kernels, per_device(): pl.pallas_call(functools.partial(kernel, n), out_shape=pltpu.VMEM((STEPS,...  38.7 us

profile of v5, /device:TPU:0, one launch (start us, length us, event | category | flops | bytes accessed | tf_op | source)
XLA Modules:
  0.0 40.6 jit_solution(2563705422589077648)
XLA Ops:
  1.3 38.7 %shard_map.91 = bf16[2,8192]{1,0:T(2,128)(2,1)S(1)} custom-call(s32[1]{0:T(128)S(6)} %copy.12.positions, s32[1]{0:T(128)S(6)} %copy.13.lengths, bf16[2,8192]{1,0:T(2,128)(2,1)} %bitcast.7, bf16[8192,512]{1,0:T(8,128)(2,1)} %wq_hbm.1, bf16[64,8192]{1,0:T(8,128)(2,1)} %bitcast.5, bf16[64,8192]{1,0:T(8,128)(2,1)} %bitcast.6, bf16[512,8192]{1,0:T(8,128)(2,1)} %wo_hbm.1, ...), custom_call_target="tpu_custom_call" | custom-call | tf_op jit(solution)/shard_map/pallas_call | solution.py:329
  40.0 0.6 %copy.11 = bf16[2,1,8192]{2,0,1:T(2,128)(2,1)} copy(bf16[2,1,8192]{2,0,1:T(2,128)(2,1)S(1)} %bitcast.4) | data formatting | bytes 65536
